TPU v7x, 32 devices: a whole 2x2x4 slice. The times are simulated.
32 devices in a mesh: sample: 8 (over y, x, core), col: 4 (over z).
Axes of the slice: x: 2, y: 2, z: 4, core: 2. Of those that a mesh axis runs over, the one named last changes fastest.
Arguments:
- block_inputs: bfloat16 [512, 17, 17, 768], P(('sample', 'col')), may hold values from 0 to 100, as said below
- first_entry: bfloat16 [1, 1, 768, 384], replicated, may hold values from -0.3125 to 0.3125
- first_wide: bfloat16 [3, 3, 192, 320], replicated, may hold values from -0.21875 to 0.21875
- first_row: bfloat16 [1, 7, 192, 192], replicated, may hold values from -0.25 to 0.25
- first_column: bfloat16 [7, 1, 192, 192], replicated, may hold values from -0.25 to 0.25
- first_reduce: bfloat16 [3, 3, 192, 192], replicated, may hold values from -0.21875 to 0.21875
- second_entry: bfloat16 [1, 1, 1280, 1152], replicated, may hold values from -0.25 to 0.25
- second_row: bfloat16 [1, 3, 384, 384], replicated, may hold values from -0.25 to 0.25
- second_column: bfloat16 [3, 1, 384, 384], replicated, may hold values from -0.25 to 0.25
- second_deep: bfloat16 [3, 3, 448, 384], replicated, may hold values from -0.125 to 0.125
- deep_row: bfloat16 [1, 3, 384, 384], replicated, may hold values from -0.25 to 0.25
- deep_column: bfloat16 [3, 1, 384, 384], replicated, may hold values from -0.25 to 0.25
- pool_project: bfloat16 [1, 1, 1280, 192], replicated, may hold values from -0.25 to 0.25
Outputs:
- feature_mean: float32 [2048], replicated
- covariance: float32 [2048, 2048], P('sample', 'col')
Inputs may be any that keep to these rules, and one draw needn't show every extreme that they name: `block_inputs`: nonnegative activations.
All inputs are finite; a program needn't handle non-finite values.
Results may differ from a plain program's by a relative error of at most 0.0003.
Values sent between devices are 32-bit elements; how exact they have to be, the bound alone decides.
A program may use at most 128 MiB of HBM per device.

v0:
```python
import jax
import jax.numpy as jnp
from jax import lax
from jax.sharding import PartitionSpec as P


def rectify(inputs, kernel, stride, padding):
    result = lax.conv_general_dilated(
        inputs,
        kernel,
        (stride, stride),
        padding,
        dimension_numbers=("NHWC", "HWIO", "NHWC"),
        preferred_element_type=jnp.float32,
    )
    return jnp.maximum(result, 0.0).astype(jnp.bfloat16)


def spatial_mean(inputs):
    return jnp.mean(inputs.astype(jnp.float32), axis=(1, 2))


def network(
    block_inputs,
    first_entry,
    first_wide,
    first_row,
    first_column,
    first_reduce,
    second_entry,
    second_row,
    second_column,
    second_deep,
    deep_row,
    deep_column,
    pool_project,
):
    no_margin = ((0, 0), (0, 0))
    entry_out = rectify(block_inputs, first_entry, 1, no_margin)
    half_width = first_wide.shape[2]
    wide_out = rectify(entry_out[..., :half_width], first_wide, 2, no_margin)
    tower_out = rectify(entry_out[..., half_width:], first_row, 1, ((0, 0), (3, 3)))
    tower_out = rectify(tower_out, first_column, 1, ((3, 3), (0, 0)))
    tower_out = rectify(tower_out, first_reduce, 2, no_margin)
    maximum = lax.reduce_window(
        block_inputs,
        jnp.array(-jnp.inf, block_inputs.dtype),
        lax.max,
        (1, 3, 3, 1),
        (1, 2, 2, 1),
        "VALID",
    )
    middle = jnp.concatenate([wide_out, tower_out, maximum], axis=3)
    second = rectify(middle, second_entry, 1, no_margin)
    branch_width = second_row.shape[2]
    deep_width = second_deep.shape[2]
    plain_width = second_entry.shape[3] - branch_width - deep_width
    plain_out = second[..., :plain_width]
    branch_in = second[..., plain_width : plain_width + branch_width]
    deep_in = second[..., plain_width + branch_width :]
    row_a = rectify(branch_in, second_row, 1, ((0, 0), (1, 1)))
    col_a = rectify(branch_in, second_column, 1, ((1, 1), (0, 0)))
    deep_out = rectify(deep_in, second_deep, 1, ((1, 1), (1, 1)))
    row_b = rectify(deep_out, deep_row, 1, ((0, 0), (1, 1)))
    col_b = rectify(deep_out, deep_column, 1, ((1, 1), (0, 0)))
    pool_pad = ((0, 0), (1, 1), (1, 1), (0, 0))
    summed = lax.reduce_window(
        middle.astype(jnp.float32),
        jnp.array(0.0, jnp.float32),
        lax.add,
        (1, 3, 3, 1),
        (1, 1, 1, 1),
        pool_pad,
    )
    ones_map = jnp.ones((1, middle.shape[1], middle.shape[2], 1), jnp.float32)
    cell_count = lax.reduce_window(
        ones_map, jnp.array(0.0, jnp.float32), lax.add, (1, 3, 3, 1), (1, 1, 1, 1), pool_pad
    )
    averaged = (summed / cell_count).astype(jnp.bfloat16)
    pooled = rectify(averaged, pool_project, 1, no_margin)
    return jnp.concatenate(
        [
            spatial_mean(plain_out),
            spatial_mean(row_a),
            spatial_mean(col_a),
            spatial_mean(row_b),
            spatial_mean(col_b),
            spatial_mean(pooled),
        ],
        axis=1,
    )


def local(
    block_inputs,
    first_entry,
    first_wide,
    first_row,
    first_column,
    first_reduce,
    second_entry,
    second_row,
    second_column,
    second_deep,
    deep_row,
    deep_column,
    pool_project,
):
    features = network(
        block_inputs,
        first_entry,
        first_wide,
        first_row,
        first_column,
        first_reduce,
        second_entry,
        second_row,
        second_column,
        second_deep,
        deep_row,
        deep_column,
        pool_project,
    )
    gathered = lax.all_gather(features, "col", axis=0, tiled=True)
    width = gathered.shape[1]
    col_width = width // lax.axis_size("col")
    col_start = lax.axis_index("col") * col_width
    row_width = width // lax.axis_size("sample")
    row_start = lax.axis_index("sample") * row_width
    group_images = gathered.shape[0]
    total_images = group_images * lax.axis_size("sample")
    highest = lax.Precision.HIGHEST
    everything = lax.all_gather(gathered, "sample", axis=0, tiled=True)
    feature_mean = jnp.sum(everything, axis=0) / total_images
    centered = everything - feature_mean
    columns = lax.dynamic_slice_in_dim(centered, col_start, col_width, 1)
    rows_part = lax.dynamic_slice_in_dim(centered, row_start, row_width, 1)
    covariance = jnp.einsum(
        "nf,nc->fc", rows_part, columns, precision=highest, preferred_element_type=jnp.float32
    ) / (total_images - 1)
    return (feature_mean, covariance)


def solution(mesh):
    placed = (
        P(("sample", "col"), None, None, None),
        P(),
        P(),
        P(),
        P(),
        P(),
        P(),
        P(),
        P(),
        P(),
        P(),
        P(),
        P(),
    )
    return jax.shard_map(
        local, mesh=mesh, in_specs=placed, out_specs=(P(), P("sample", "col")), check_vma=False
    )
```

profile of v0, /device:TPU:0, one launch (start us, length us, event | category | flops | bytes accessed | tf_op | source)
XLA Modules:
  0.0 136.8 jit_solution(5482810569288663354)
XLA Ops:
  7.2 0.0 all-gather.2.cloned.1.call-start
  7.2 5.7 %fusion.25 = bf16[16,8,8,768]{3,0,2,1:T(8,128)(2,1)} fusion(bf16[16,17,17,768]{3,0,2,1:T(8,128)(2,1)} %param.13), kind=kOutput, calls=%fused_computation.47 | output fusion | flops 6291456 | bytes 8675328 | tf_op jit(solution)/shard_map/reduce_window | solution.py:45
  12.9 4.1 %maximum_convert_fusion = bf16[16,17,17,384]{3,0,2,1:T(8,128)(2,1)S(1)} fusion(bf16[16,17,17,768]{3,0,2,1:T(8,128)(2,1)S(1)} %copy-done.2, bf16[1,1,768,384]{3,2,1,0:T(8,128)(2,1)S(1)} %copy-done.11), kind=kOutput, calls=%fused_computation | convolution fusion | flops 2730897408 | bytes 11243520 | tf_op jit(solution)/shard_map/conv_general_dilated | solution.py:8
  17.1 11.7 %fusion.6 = bf16[16,17,17,192]{3,0,2,1:T(8,128)(2,1)} fusion(bf16[1,7,192,192]{3,2,1,0:T(8,128)(2,1)S(1)} %copy-done.10, bf16[16,17,17,384]{3,0,2,1:T(8,128)(2,1)S(1)} %maximum_convert_fusion), kind=kOutput, calls=%fused_computation.9 | convolution fusion | flops 2145779712 | bytes 4831232 | tf_op jit(solution)/shard_map/conv_general_dilated | solution.py:8
  28.7 3.0 %maximum_convert_fusion.11 = bf16[16,8,8,320]{3,0,2,1:T(8,128)(2,1)} fusion(bf16[3,3,192,320]{3,2,1,0:T(8,128)(2,1)S(1)} %copy-done.5, bf16[16,17,17,384]{3,0,2,1:T(8,128)(2,1)S(1)} %maximum_convert_fusion), kind=kOutput, calls=%fused_computation.25 | convolution fusion | flops 1133117440 | bytes 4349952 | tf_op jit(solution)/shard_map/conv_general_dilated | solution.py:8
  31.7 9.4 %fusion.13 = bf16[16,8,8,192]{3,0,2,1:T(8,128)(2,1)} fusion(bf16[3,3,192,192]{3,2,1,0:T(8,128)(2,1)} %param.18, bf16[7,1,192,192]{3,2,1,0:T(8,128)(2,1)} %param.17, bf16[16,17,17,192]{3,0,2,1:T(8,128)(2,1)} %fusion.6), kind=kOutput, calls=%fused_computation.28 | convolution fusion | flops 2830089216 | bytes 3348480 | tf_op jit(solution)/shard_map/conv_general_dilated | solution.py:8
  41.1 5.4 %concatenate.6 = bf16[16,8,8,1280]{3,0,2,1:T(8,128)(2,1)} concatenate(bf16[16,8,8,320]{3,0,2,1:T(8,128)(2,1)} %maximum_convert_fusion.11, bf16[16,8,8,192]{3,0,2,1:T(8,128)(2,1)} %fusion.13, bf16[16,8,8,768]{3,0,2,1:T(8,128)(2,1)} %fusion.25), dimensions={3} | concatenate | bytes 5242880 | tf_op jit(solution)/shard_map/concatenate | solution.py:53
  46.5 6.2 %fusion.4 = bf16[16,8,8,1152]{3,0,2,1:T(8,128)(2,1)S(1)} fusion(bf16[16,8,8,1280]{3,0,2,1:T(8,128)(2,1)} %concatenate.6, bf16[1,1,1280,1152]{3,2,1,0:T(8,128)(2,1)} %param.19), kind=kOutput, calls=%fused_computation.7 | convolution fusion | flops 3022258176 | bytes 7929856 | tf_op jit(solution)/shard_map/conv_general_dilated | solution.py:8
  52.7 0.2 convert_reduce_fusion.4
  52.9 4.6 %maximum_convert_fusion.8 = bf16[16,8,8,384]{3,0,2,1:T(8,128)(2,1)S(1)} fusion(bf16[3,3,448,384]{3,2,1,0:T(8,128)(2,1)S(1)} %copy-done, bf16[16,8,8,1152]{3,0,2,1:T(8,128)(2,1)S(1)} %fusion.4), kind=kOutput, calls=%fused_computation.19 | convolution fusion | flops 2665218048 | bytes 4931584 | tf_op jit(solution)/shard_map/conv_general_dilated | solution.py:8
  57.5 1.5 %convert_reduce_fusion = f32[16,384]{1,0:T(8,128)S(1)} fusion(bf16[16,8,8,384]{3,0,2,1:T(8,128)(2,1)S(1)} %maximum_convert_fusion.8, bf16[3,1,384,384]{3,2,1,0:T(8,128)(2,1)S(1)} %copy-done.6), kind=kOutput, calls=%fused_computation.15 | convolution fusion | flops 832038912 | bytes 1695744 | tf_op jit(solution)/shard_map/conv_general_dilated | solution.py:8
  59.0 1.5 %convert_reduce_fusion.1 = f32[16,384]{1,0:T(8,128)S(1)} fusion(bf16[16,8,8,384]{3,0,2,1:T(8,128)(2,1)S(1)} %maximum_convert_fusion.8, bf16[1,3,384,384]{3,2,1,0:T(8,128)(2,1)S(1)} %copy-done.7), kind=kOutput, calls=%fused_computation.17 | convolution fusion | flops 832038912 | bytes 1695744 | tf_op jit(solution)/shard_map/conv_general_dilated | solution.py:8
  60.4 1.5 %convert_reduce_fusion.2 = f32[16,384]{1,0:T(8,128)S(1)} fusion(bf16[3,1,384,384]{3,2,1,0:T(8,128)(2,1)S(1)} %copy-done.8, bf16[16,8,8,1152]{3,0,2,1:T(8,128)(2,1)S(1)} %fusion.4), kind=kOutput, calls=%fused_computation.20 | convolution fusion | flops 832038912 | bytes 1695744 | tf_op jit(solution)/shard_map/conv_general_dilated | solution.py:8
  62.0 1.5 %convert_reduce_fusion.3 = f32[16,384]{1,0:T(8,128)S(1)} fusion(bf16[1,3,384,384]{3,2,1,0:T(8,128)(2,1)S(1)} %copy-done.9, bf16[16,8,8,1152]{3,0,2,1:T(8,128)(2,1)S(1)} %fusion.4), kind=kOutput, calls=%fused_computation.22 | convolution fusion | flops 832038912 | bytes 1695744 | tf_op jit(solution)/shard_map/conv_general_dilated | solution.py:8
  63.5 0.2 copy-done.1
  63.7 1.6 %multiply_convert_fusion = bf16[16,8,8,1280]{3,0,2,1:T(8,128)(2,1)S(1)} fusion(bf16[16,8,8,1280]{3,0,2,1:T(8,128)(2,1)S(1)} %copy-done.1, f32[8,8]{1,0:T(8,128)S(1)} %copy-done.4), kind=kOutput, calls=%fused_computation.1 | output fusion | flops 14417920 | bytes 5243136 | tf_op jit(solution)/shard_map/reduce_window | solution.py:67
  65.3 0.9 fusion.16
  66.2 0.1 concatenate.7
  66.3 18.0 %all_gather.6 = f32[64,2048]{1,0:T(8,128)} all-gather(f32[16,2048]{1,0:T(8,128)S(1)} %concatenate.7), channel_id=1, replica_groups=mesh['sample'=8,'col'=4] {'col'}, dimensions={0}, use_global_device_ids=true | all-gather | bytes 655360 | tf_op jit(solution)/shard_map/all_gather | solution.py:124
  84.3 0.0 all-gather.2.cloned.1.call-update
  84.3 38.7 %all-gather.2.cloned.1.call-done = f32[512,2048]{1,0:T(8,128)} async-done(((f32[64,2048]{1,0:T(8,128)}), f32[512,2048]{1,0:T(8,128)}) %all-gather.2.cloned.1.call-update) | async-done | bytes 4194320 | tf_op jit(solution)/shard_map/all_gather | solution.py:133
  123.1 2.4 %reduce_sum.69 = f32[2048]{0:T(1024)S(1)} reduce(f32[512,2048]{1,0:T(8,128)} %all-gather.2.cloned.1.call-done, f32[]{:T(128)} %constant.14.clone.1), dimensions={0}, to_apply=%region_8.0 | reduce | flops 1046528 | bytes 4202500 | tf_op jit(solution)/shard_map/reduce_sum | solution.py:134
  125.5 2.6 %broadcast_subtract_fusion = f32[512,2048]{1,0:T(8,128)S(1)} fusion(f32[512,2048]{1,0:T(8,128)} %all-gather.2.cloned.1.call-done, f32[2048]{0:T(1024)S(1)} %broadcast_multiply_fusion.6), kind=kLoop, calls=%fused_computation.14 | loop fusion | flops 1048576 | bytes 8396800 | tf_op jit(solution)/shard_map/sub | solution.py:135
  128.1 1.9 %convolution_multiply_fusion = f32[256,512]{1,0:T(8,128)} fusion(f32[512,2048]{1,0:T(8,128)S(1)} %broadcast_subtract_fusion, s32[]{:T(128)S(6)} %select_n.7, s32[]{:T(128)S(6)} %select_n.6), kind=kOutput, calls=%fused_computation.32 | convolution fusion | flops 805437440 | bytes 2097160 | tf_op jit(solution)/shard_map/nf,nc->fc/dot_general | solution.py:138
  (30 shorter events, 0.1 us)
Async XLA Ops:
  7.2 45.7 %copy-start = (bf16[3,3,448,384]{3,2,1,0:T(8,128)(2,1)S(1)}, bf16[3,3,448,384]{3,2,1,0:T(8,128)(2,1)}, u32[]{:S(2)}) copy-start(bf16[3,3,448,384]{3,2,1,0:T(8,128)(2,1)} %param.22) | copy-start | bytes 9289732
  7.2 115.9 %all-gather.2.cloned.1.call-start = ((), (), s32[]{:S(2)}) async-start(), calls=%async_computation | async-start | bytes 4718592 | tf_op jit(solution)/shard_map/all_gather | solution.py:133
  7.2 5.7 %copy-start.2 = (bf16[16,17,17,768]{3,0,2,1:T(8,128)(2,1)S(1)}, bf16[16,17,17,768]{3,0,2,1:T(8,128)(2,1)}, u32[]{:S(2)}) copy-start(bf16[16,17,17,768]{3,0,2,1:T(8,128)(2,1)} %param.13) | copy-start | bytes 21307396
  7.2 5.7 %copy-start.11 = (bf16[1,1,768,384]{3,2,1,0:T(8,128)(2,1)S(1)}, bf16[1,1,768,384]{3,2,1,0:T(8,128)(2,1)}, u32[]{:S(2)}) copy-start(bf16[1,1,768,384]{3,2,1,0:T(8,128)(2,1)} %param.14) | copy-start | bytes 1769476
  12.9 4.1 %copy-start.10 = (bf16[1,7,192,192]{3,2,1,0:T(8,128)(2,1)S(1)}, bf16[1,7,192,192]{3,2,1,0:T(8,128)(2,1)}, u32[]{:S(2)}) copy-start(bf16[1,7,192,192]{3,2,1,0:T(8,128)(2,1)} %param.16) | copy-start | bytes 1548292
  17.1 11.7 %copy-start.5 = (bf16[3,3,192,320]{3,2,1,0:T(8,128)(2,1)S(1)}, bf16[3,3,192,320]{3,2,1,0:T(8,128)(2,1)}, u32[]{:S(2)}) copy-start(bf16[3,3,192,320]{3,2,1,0:T(8,128)(2,1)} %param.15) | copy-start | bytes 3317764
  52.9 4.6 %copy-start.6 = (bf16[3,1,384,384]{3,2,1,0:T(8,128)(2,1)S(1)}, bf16[3,1,384,384]{3,2,1,0:T(8,128)(2,1)}, u32[]{:S(2)}) copy-start(bf16[3,1,384,384]{3,2,1,0:T(8,128)(2,1)} %param.24) | copy-start | bytes 2654212
  57.5 1.5 %copy-start.7 = (bf16[1,3,384,384]{3,2,1,0:T(8,128)(2,1)S(1)}, bf16[1,3,384,384]{3,2,1,0:T(8,128)(2,1)}, u32[]{:S(2)}) copy-start(bf16[1,3,384,384]{3,2,1,0:T(8,128)(2,1)} %param.23) | copy-start | bytes 2654212
  58.9 1.5 %copy-start.8 = (bf16[3,1,384,384]{3,2,1,0:T(8,128)(2,1)S(1)}, bf16[3,1,384,384]{3,2,1,0:T(8,128)(2,1)}, u32[]{:S(2)}) copy-start(bf16[3,1,384,384]{3,2,1,0:T(8,128)(2,1)} %param.21) | copy-start | bytes 2654212
  60.4 1.5 %copy-start.9 = (bf16[1,3,384,384]{3,2,1,0:T(8,128)(2,1)S(1)}, bf16[1,3,384,384]{3,2,1,0:T(8,128)(2,1)}, u32[]{:S(2)}) copy-start(bf16[1,3,384,384]{3,2,1,0:T(8,128)(2,1)} %param.20) | copy-start | bytes 2654212
  62.0 1.7 %copy-start.1 = (bf16[16,8,8,1280]{3,0,2,1:T(8,128)(2,1)S(1)}, bf16[16,8,8,1280]{3,0,2,1:T(8,128)(2,1)}, u32[]{:S(2)}) copy-start(bf16[16,8,8,1280]{3,0,2,1:T(8,128)(2,1)} %concatenate.6) | copy-start | bytes 7864324
  62.0 1.7 %copy-start.4 = (f32[8,8]{1,0:T(8,128)S(1)}, f32[8,8]{1,0:T(8,128)}, u32[]{:S(2)}) copy-start(f32[8,8]{1,0:T(8,128)} %constant.17.clone.1) | copy-start | bytes 772
  63.7 1.6 %copy-start.12 = (bf16[1,1,1280,192]{2,3,1,0:T(8,128)(2,1)S(1)}, bf16[1,1,1280,192]{2,3,1,0:T(8,128)(2,1)}, u32[]{:S(2)}) copy-start(bf16[1,1,1280,192]{2,3,1,0:T(8,128)(2,1)} %param.25) | copy-start | bytes 1474564
  125.5 2.6 %copy-start.3 = (f32[2048]{0:T(1024)}, f32[2048]{0:T(1024)S(1)}, u32[]{:S(2)}) copy-start(f32[2048]{0:T(1024)S(1)} %broadcast_multiply_fusion.6) | copy-start | bytes 24580
Sparse Core Ops, SparseCore 0:
  84.5 38.5 all-gather.1
where the time goes:
time: 137 us
  matrix products  47.6 us (35%)
  waiting for transfers between devices  38.7 us (28%)
  blocking collectives  18 us (13%)
  between operations  14.3 us (10%)
  other arithmetic  12.5 us (9%)
  local copies, waits for them, and re-layouts  5.73 us (4%)
    conv_general_dilated x11, matrix products, rectify(): lax.conv_general_dilated(inputs, kernel, (stride, stride), padding, dimen...  45.7 us
    all_gather x1, waiting for transfers between devices, local(): everything = lax.all_gather(gathered, 'sample', axis=0, tiled=True)  38.7 us
    all_gather x1, blocking collectives, local(): gathered = lax.all_gather(features, 'col', axis=0, tiled=True)  18 us
    another operation x1, other arithmetic, network(): lax.reduce_window(block_inputs, jnp.array(-jnp.inf, block_inputs.dtype),...  5.68 us
    concatenate x1, local copies, waits for them, and re-layouts, network(): middle = jnp.concatenate([wide_out, tower_out, maximum], axis=3)  5.38 us
  transfers between devices with their start and end apart: 1, of which 1 were waited for; matrix products, arithmetic and copies ran while one was open for 0% of the time, Pallas kernels for 0%

commit v1 on v0

--- a/solution.py
+++ b/solution.py
@@ -1,6 +1,10 @@
+import functools
+
 import jax
 import jax.numpy as jnp
 from jax import lax
+from jax.experimental import pallas as pl
+from jax.experimental.pallas import tpu as pltpu
 from jax.sharding import PartitionSpec as P
 
 
@@ -91,6 +95,173 @@
     )
 
 
+def exchange_kernel(
+    n_sample,
+    n_col,
+    feats_ref,
+    mean_ref,
+    cov_ref,
+    cols,
+    rows,
+    sums_col,
+    sums_sample,
+    col_send,
+    col_recv,
+    row_send,
+    row_recv,
+    sum_send,
+    sum_recv,
+    cols_send,
+    cols_recv,
+    rows_send,
+    rows_recv,
+    total_send,
+    total_recv,
+):
+    s = lax.axis_index("sample")
+    c = lax.axis_index("col")
+    images = feats_ref.shape[0]
+    col_width = cols.shape[3]
+    row_width = rows.shape[3]
+    total_images = images * n_sample * n_col
+    mesh_id = pl.DeviceIdType.MESH
+
+    def col_at(index):
+        return pl.ds(pl.multiple_of(index * col_width, 128), col_width)
+
+    def row_at(index):
+        return pl.ds(pl.multiple_of(index * row_width, 128), row_width)
+
+    def send(source, target, send_sem, recv_sem, sample, col):
+        copy = pltpu.make_async_remote_copy(
+            src_ref=source,
+            dst_ref=target,
+            send_sem=send_sem,
+            recv_sem=recv_sem,
+            device_id=(sample, col),
+            device_id_type=mesh_id,
+        )
+        copy.start()
+        return copy
+
+    barrier = pltpu.get_barrier_semaphore()
+    for k in range(1, n_col):
+        pl.semaphore_signal(
+            barrier, inc=1, device_id=(s, lax.rem(c + k, n_col)), device_id_type=mesh_id
+        )
+    for k in range(1, n_sample):
+        pl.semaphore_signal(
+            barrier, inc=1, device_id=(lax.rem(s + k, n_sample), c), device_id_type=mesh_id
+        )
+    sums_col[c] = jnp.sum(feats_ref[...], axis=0, keepdims=True)
+    cols[s, c] = feats_ref[:, col_at(c)]
+    rows[s, c] = feats_ref[:, row_at(s)]
+    pl.semaphore_wait(barrier, n_col - 1 + n_sample - 1)
+
+    sends = []
+    first_cols, first_sums, first_rows = [], [], []
+    for k in range(1, n_col):
+        to = lax.rem(c + k, n_col)
+        first_cols.append(
+            send(feats_ref.at[:, col_at(to)], cols.at[s, c], col_send.at[k], col_recv.at[k], s, to)
+        )
+        first_sums.append(
+            send(sums_col.at[c], sums_col.at[c], sum_send.at[k], sum_recv.at[k], s, to)
+        )
+    for k in range(1, n_sample):
+        to = lax.rem(s + k, n_sample)
+        first_rows.append(
+            send(feats_ref.at[:, row_at(to)], rows.at[s, c], row_send.at[k], row_recv.at[k], to, c)
+        )
+    for copy in first_rows:
+        copy.wait_recv()
+    second_rows = []
+    for k in range(1, n_col):
+        to = lax.rem(c + k, n_col)
+        second_rows.append(
+            send(rows.at[:, c], rows.at[:, c], rows_send.at[k], rows_recv.at[k], s, to)
+        )
+    for copy in first_cols:
+        copy.wait_recv()
+    second_cols = []
+    for k in range(1, n_sample):
+        to = lax.rem(s + k, n_sample)
+        second_cols.append(
+            send(cols.at[s], cols.at[s], cols_send.at[k], cols_recv.at[k], to, c)
+        )
+    for copy in first_sums:
+        copy.wait_recv()
+    sums_sample[s] = jnp.sum(sums_col[...], axis=0)
+    second_sums = []
+    for k in range(1, n_sample):
+        to = lax.rem(s + k, n_sample)
+        second_sums.append(
+            send(sums_sample.at[s], sums_sample.at[s], total_send.at[k], total_recv.at[k], to, c)
+        )
+    for copy in second_sums:
+        copy.wait_recv()
+    mean_ref[...] = jnp.sum(sums_sample[...], axis=0) * (1.0 / total_images)
+    for copy in second_rows:
+        copy.wait_recv()
+    row_values = rows[...].reshape(total_images, row_width) - mean_ref[:, row_at(s)]
+    row_values = row_values.T
+    row_high = row_values.astype(jnp.bfloat16)
+    row_low = (row_values - row_high.astype(jnp.float32)).astype(jnp.bfloat16)
+    for copy in second_cols:
+        copy.wait_recv()
+    col_values = cols[...].reshape(total_images, col_width) - mean_ref[:, col_at(c)]
+    col_high = col_values.astype(jnp.bfloat16)
+    col_low = (col_values - col_high.astype(jnp.float32)).astype(jnp.bfloat16)
+    product = jnp.dot(row_high, col_low, preferred_element_type=jnp.float32)
+    product += jnp.dot(row_low, col_high, preferred_element_type=jnp.float32)
+    product += jnp.dot(row_high, col_high, preferred_element_type=jnp.float32)
+    cov_ref[...] = product * (1.0 / (total_images - 1))
+    for copy in first_cols + first_sums + first_rows + second_rows + second_cols + second_sums:
+        copy.wait_send()
+
+
+def exchange(features):
+    n_sample = lax.axis_size("sample")
+    n_col = lax.axis_size("col")
+    images, width = features.shape
+    row_width = width // n_sample
+    col_width = width // n_col
+    dma = pltpu.SemaphoreType.DMA
+    vmem = pl.BlockSpec(memory_space=pltpu.VMEM)
+    mean, covariance = pl.pallas_call(
+        functools.partial(exchange_kernel, n_sample, n_col),
+        out_shape=(
+            jax.ShapeDtypeStruct((1, width), jnp.float32),
+            jax.ShapeDtypeStruct((row_width, col_width), jnp.float32),
+        ),
+        in_specs=[vmem],
+        out_specs=(vmem, vmem),
+        scratch_shapes=[
+            pltpu.VMEM((n_sample, n_col, images, col_width), jnp.float32),
+            pltpu.VMEM((n_sample, n_col, images, row_width), jnp.float32),
+            pltpu.VMEM((n_col, 1, width), jnp.float32),
+            pltpu.VMEM((n_sample, 1, width), jnp.float32),
+            dma((n_col,)),
+            dma((n_col,)),
+            dma((n_sample,)),
+            dma((n_sample,)),
+            dma((n_col,)),
+            dma((n_col,)),
+            dma((n_sample,)),
+            dma((n_sample,)),
+            dma((n_col,)),
+            dma((n_col,)),
+            dma((n_sample,)),
+            dma((n_sample,)),
+        ],
+        compiler_params=pltpu.CompilerParams(
+            collective_id=0, has_side_effects=True, vmem_limit_bytes=48 * 1024 * 1024
+        ),
+        name="exchange",
+    )(features)
+    return mean.reshape(width), covariance
+
+
 def local(
     block_inputs,
     first_entry,
@@ -121,24 +292,7 @@
         deep_column,
         pool_project,
     )
-    gathered = lax.all_gather(features, "col", axis=0, tiled=True)
-    width = gathered.shape[1]
-    col_width = width // lax.axis_size("col")
-    col_start = lax.axis_index("col") * col_width
-    row_width = width // lax.axis_size("sample")
-    row_start = lax.axis_index("sample") * row_width
-    group_images = gathered.shape[0]
-    total_images = group_images * lax.axis_size("sample")
-    highest = lax.Precision.HIGHEST
-    everything = lax.all_gather(gathered, "sample", axis=0, tiled=True)
-    feature_mean = jnp.sum(everything, axis=0) / total_images
-    centered = everything - feature_mean
-    columns = lax.dynamic_slice_in_dim(centered, col_start, col_width, 1)
-    rows_part = lax.dynamic_slice_in_dim(centered, row_start, row_width, 1)
-    covariance = jnp.einsum(
-        "nf,nc->fc", rows_part, columns, precision=highest, preferred_element_type=jnp.float32
-    ) / (total_images - 1)
-    return (feature_mean, covariance)
+    return exchange(features)
 
 
 def solution(mesh):

time: 137 us -> 92.6 us (0.68)
  waiting for transfers between devices: 38.7 us -> 0 us
  Pallas kernels: 0 us -> 24.7 us
  blocking collectives: 18 us -> 0 us
  between operations: 14.3 us -> 0.88 us
  other arithmetic: 12.5 us -> 7.28 us
  matrix products: 47.6 us -> 50.8 us
  local copies, waits for them, and re-layouts: 5.73 us -> 8.69 us
    all_gather x1 -> x0, waiting for transfers between devices: 38.7 us -> none  [local(): everything = lax.all_gather(gathered, 'sample', axis=0, tiled=True)]
    pallas_call x0 -> x1, Pallas kernels: none -> 24.7 us  [exchange(): pl.pallas_call(functools.partial(exchange_kernel, n_sample, n_col), out_s...]
    all_gather x1 -> x0, blocking collectives: 18 us -> none  [local(): gathered = lax.all_gather(features, 'col', axis=0, tiled=True)]
    conv_general_dilated x11, matrix products: 45.7 us -> 50.8 us  [rectify(): lax.conv_general_dilated(inputs, kernel, (stride, stride), padding, dimen...]
    unnamed x26 -> x22, local copies, waits for them, and re-layouts: 0.24 us -> 3.2 us
    sub x1 -> x0, other arithmetic: 2.61 us -> none  [local(): centered = everything - feature_mean]
    reduce_sum x1 -> x0, other arithmetic: 2.41 us -> none  [local(): feature_mean = jnp.sum(everything, axis=0) / total_images]
    dot_general x1 -> x0, matrix products: 1.87 us -> none  [local(): jnp.einsum('nf,nc->fc', rows_part, columns, precision=highest, preferred_...]
  transfers between devices with their start and end apart: 1 -> 0, of which waited for: 1 -> 0; matrix products, arithmetic and copies ran while one was open for 0% -> 0% of each run, Pallas kernels for 0% -> 0%
where the time goes in v1:
time: 92.6 us; the launch traced here: 92.3 us
  matrix products  50.8 us (55%)
  Pallas kernels  24.7 us (27%)
  local copies, waits for them, and re-layouts  8.69 us (9%)
  other arithmetic  7.28 us (8%)
    conv_general_dilated x11, matrix products, rectify(): lax.conv_general_dilated(inputs, kernel, (stride, stride), padding, dimen...  50.8 us
    pallas_call x1, Pallas kernels, exchange(): pl.pallas_call(functools.partial(exchange_kernel, n_sample, n_col), out_s...  24.7 us
    another operation x1, other arithmetic, network(): lax.reduce_window(block_inputs, jnp.array(-jnp.inf, block_inputs.dtype),...  5.53 us
    concatenate x1, local copies, waits for them, and re-layouts, network(): middle = jnp.concatenate([wide_out, tower_out, maximum], axis=3)  5.38 us
    unnamed x22, local copies, waits for them, and re-layouts  3.2 us

profile of v1, /device:TPU:0, one launch (start us, length us, event | category | flops | bytes accessed | tf_op | source)
XLA Modules:
  0.0 92.3 jit_solution(13360253014131977233)
XLA Ops:
  0.6 0.0 copy-start
  0.7 7.1 %maximum_convert_fusion = bf16[16,17,17,384]{3,0,2,1:T(8,128)(2,1)S(1)} fusion(bf16[16,17,17,768]{3,0,2,1:T(8,128)(2,1)} %param.13, bf16[1,1,768,384]{3,2,1,0:T(8,128)(2,1)} %param.14), kind=kOutput, calls=%fused_computation | convolution fusion | flops 2730897408 | bytes 11243520 | tf_op jit(solution)/shard_map/conv_general_dilated | solution.py:12
  7.8 1.7 %copy-done.9 = bf16[16,17,17,384]{3,0,2,1:T(8,128)(2,1)} copy-done((bf16[16,17,17,384]{3,0,2,1:T(8,128)(2,1)}, bf16[16,17,17,384]{3,0,2,1:T(8,128)(2,1)S(1)}, u32[]{:S(2)}) %copy-start.9) | copy-done | bytes 3551256
  9.5 11.7 %fusion.6 = bf16[16,17,17,192]{3,0,2,1:T(8,128)(2,1)} fusion(bf16[1,7,192,192]{3,2,1,0:T(8,128)(2,1)S(1)} %copy-done.7, bf16[16,17,17,384]{3,0,2,1:T(8,128)(2,1)S(1)} %maximum_convert_fusion), kind=kOutput, calls=%fused_computation.9 | convolution fusion | flops 2145779712 | bytes 4831232 | tf_op jit(solution)/shard_map/conv_general_dilated | solution.py:12
  21.2 9.4 %fusion.13 = bf16[16,8,8,192]{3,0,2,1:T(8,128)(2,1)} fusion(bf16[3,3,192,192]{3,2,1,0:T(8,128)(2,1)} %param.18, bf16[7,1,192,192]{3,2,1,0:T(8,128)(2,1)} %param.17, bf16[16,17,17,192]{3,0,2,1:T(8,128)(2,1)} %fusion.6), kind=kOutput, calls=%fused_computation.27 | convolution fusion | flops 2830089216 | bytes 3348480 | tf_op jit(solution)/shard_map/conv_general_dilated | solution.py:12
  30.6 5.0 %maximum_convert_fusion.11 = bf16[16,8,8,320]{3,0,2,1:T(8,128)(2,1)} fusion(bf16[3,3,192,320]{3,2,1,0:T(8,128)(2,1)} %param.15, bf16[16,17,17,384]{3,0,2,1:T(8,128)(2,1)} %copy-done.9), kind=kOutput, calls=%fused_computation.24 | convolution fusion | flops 1133117440 | bytes 4349952 | tf_op jit(solution)/shard_map/conv_general_dilated | solution.py:12
  35.6 5.5 %fusion.22 = bf16[16,8,8,768]{3,0,2,1:T(8,128)(2,1)} fusion(bf16[16,17,17,768]{3,0,2,1:T(8,128)(2,1)} %param.13), kind=kOutput, calls=%fused_computation.41 | output fusion | flops 6291456 | bytes 8675328 | tf_op jit(solution)/shard_map/reduce_window | solution.py:49
  41.2 5.4 %concatenate.6 = bf16[16,8,8,1280]{3,0,2,1:T(8,128)(2,1)} concatenate(bf16[16,8,8,320]{3,0,2,1:T(8,128)(2,1)} %maximum_convert_fusion.11, bf16[16,8,8,192]{3,0,2,1:T(8,128)(2,1)} %fusion.13, bf16[16,8,8,768]{3,0,2,1:T(8,128)(2,1)} %fusion.22), dimensions={3} | concatenate | bytes 5242880 | tf_op jit(solution)/shard_map/concatenate | solution.py:57
  46.5 6.2 %fusion.4 = bf16[16,8,8,1152]{3,0,2,1:T(8,128)(2,1)S(1)} fusion(bf16[16,8,8,1280]{3,0,2,1:T(8,128)(2,1)} %concatenate.6, bf16[1,1,1280,1152]{3,2,1,0:T(8,128)(2,1)} %param.19), kind=kOutput, calls=%fused_computation.7 | convolution fusion | flops 3022258176 | bytes 7929856 | tf_op jit(solution)/shard_map/conv_general_dilated | solution.py:12
  52.7 0.0 copy-start.3
  52.7 4.6 %maximum_convert_fusion.8 = bf16[16,8,8,384]{3,0,2,1:T(8,128)(2,1)S(1)} fusion(bf16[3,3,448,384]{3,2,1,0:T(8,128)(2,1)S(1)} %copy-done, bf16[16,8,8,1152]{3,0,2,1:T(8,128)(2,1)S(1)} %fusion.4), kind=kOutput, calls=%fused_computation.18 | convolution fusion | flops 2665218048 | bytes 4931584 | tf_op jit(solution)/shard_map/conv_general_dilated | solution.py:12
  57.3 1.5 %convert_reduce_fusion = f32[16,384]{1,0:T(8,128)S(1)} fusion(bf16[16,8,8,384]{3,0,2,1:T(8,128)(2,1)S(1)} %maximum_convert_fusion.8, bf16[3,1,384,384]{3,2,1,0:T(8,128)(2,1)S(1)} %copy-done.3), kind=kOutput, calls=%fused_computation.14 | convolution fusion | flops 832038912 | bytes 1695744 | tf_op jit(solution)/shard_map/conv_general_dilated | solution.py:12
  58.8 0.0 copy-start.5
  58.8 1.5 %convert_reduce_fusion.1 = f32[16,384]{1,0:T(8,128)S(1)} fusion(bf16[16,8,8,384]{3,0,2,1:T(8,128)(2,1)S(1)} %maximum_convert_fusion.8, bf16[1,3,384,384]{3,2,1,0:T(8,128)(2,1)S(1)} %copy-done.4), kind=kOutput, calls=%fused_computation.16 | convolution fusion | flops 832038912 | bytes 1695744 | tf_op jit(solution)/shard_map/conv_general_dilated | solution.py:12
  60.3 1.5 %convert_reduce_fusion.2 = f32[16,384]{1,0:T(8,128)S(1)} fusion(bf16[3,1,384,384]{3,2,1,0:T(8,128)(2,1)S(1)} %copy-done.5, bf16[16,8,8,1152]{3,0,2,1:T(8,128)(2,1)S(1)} %fusion.4), kind=kOutput, calls=%fused_computation.19 | convolution fusion | flops 832038912 | bytes 1695744 | tf_op jit(solution)/shard_map/conv_general_dilated | solution.py:12
  61.8 0.0 copy-start.2
  61.9 1.5 %convert_reduce_fusion.3 = f32[16,384]{1,0:T(8,128)S(1)} fusion(bf16[1,3,384,384]{3,2,1,0:T(8,128)(2,1)S(1)} %copy-done.6, bf16[16,8,8,1152]{3,0,2,1:T(8,128)(2,1)S(1)} %fusion.4), kind=kOutput, calls=%fused_computation.21 | convolution fusion | flops 832038912 | bytes 1695744 | tf_op jit(solution)/shard_map/conv_general_dilated | solution.py:12
  63.4 0.2 convert_reduce_fusion.4
  63.6 1.6 %multiply_convert_fusion = bf16[16,8,8,1280]{3,0,2,1:T(8,128)(2,1)S(1)} fusion(bf16[16,8,8,1280]{3,0,2,1:T(8,128)(2,1)S(1)} %copy-done.1, f32[8,8]{1,0:T(8,128)S(1)} %copy-done.2), kind=kOutput, calls=%fused_computation.1 | output fusion | flops 14417920 | bytes 5243136 | tf_op jit(solution)/shard_map/reduce_window | solution.py:71
  65.2 0.9 fusion.16
  66.1 0.1 concatenate.7.feats_ref
  66.2 24.7 %exchange.1 = (f32[1,2048]{1,0:T(1,128)S(1)}, f32[256,512]{1,0:T(8,128)S(1)}) custom-call(f32[16,2048]{1,0:T(8,128)S(1)} %concatenate.7.feats_ref), custom_call_target="tpu_custom_call" | custom-call | tf_op jit(solution)/shard_map/exchange/pallas_call | solution.py:231
  90.9 0.6 copy.17
  91.5 0.8 copy.18
  (19 shorter events, 0.1 us)
Async XLA Ops:
  0.6 52.1 %copy-start = (bf16[3,3,448,384]{3,2,1,0:T(8,128)(2,1)S(1)}, bf16[3,3,448,384]{3,2,1,0:T(8,128)(2,1)}, u32[]{:S(2)}) copy-start(bf16[3,3,448,384]{3,2,1,0:T(8,128)(2,1)} %param.22) | copy-start | bytes 9289732
  0.6 8.9 %copy-start.7 = (bf16[1,7,192,192]{3,2,1,0:T(8,128)(2,1)S(1)}, bf16[1,7,192,192]{3,2,1,0:T(8,128)(2,1)}, u32[]{:S(2)}) copy-start(bf16[1,7,192,192]{3,2,1,0:T(8,128)(2,1)} %param.16) | copy-start | bytes 1548292
  7.8 1.8 %copy-start.9 = (bf16[16,17,17,384]{3,0,2,1:T(8,128)(2,1)}, bf16[16,17,17,384]{3,0,2,1:T(8,128)(2,1)S(1)}, u32[]{:S(2)}) copy-start(bf16[16,17,17,384]{3,0,2,1:T(8,128)(2,1)S(1)} %maximum_convert_fusion) | copy-start | bytes 10653700
  52.7 4.6 %copy-start.3 = (bf16[3,1,384,384]{3,2,1,0:T(8,128)(2,1)S(1)}, bf16[3,1,384,384]{3,2,1,0:T(8,128)(2,1)}, u32[]{:S(2)}) copy-start(bf16[3,1,384,384]{3,2,1,0:T(8,128)(2,1)} %param.24) | copy-start | bytes 2654212
  57.3 1.5 %copy-start.4 = (bf16[1,3,384,384]{3,2,1,0:T(8,128)(2,1)S(1)}, bf16[1,3,384,384]{3,2,1,0:T(8,128)(2,1)}, u32[]{:S(2)}) copy-start(bf16[1,3,384,384]{3,2,1,0:T(8,128)(2,1)} %param.23) | copy-start | bytes 2654212
  58.8 1.5 %copy-start.5 = (bf16[3,1,384,384]{3,2,1,0:T(8,128)(2,1)S(1)}, bf16[3,1,384,384]{3,2,1,0:T(8,128)(2,1)}, u32[]{:S(2)}) copy-start(bf16[3,1,384,384]{3,2,1,0:T(8,128)(2,1)} %param.21) | copy-start | bytes 2654212
  60.3 1.5 %copy-start.6 = (bf16[1,3,384,384]{3,2,1,0:T(8,128)(2,1)S(1)}, bf16[1,3,384,384]{3,2,1,0:T(8,128)(2,1)}, u32[]{:S(2)}) copy-start(bf16[1,3,384,384]{3,2,1,0:T(8,128)(2,1)} %param.20) | copy-start | bytes 2654212
  61.8 1.7 %copy-start.1 = (bf16[16,8,8,1280]{3,0,2,1:T(8,128)(2,1)S(1)}, bf16[16,8,8,1280]{3,0,2,1:T(8,128)(2,1)}, u32[]{:S(2)}) copy-start(bf16[16,8,8,1280]{3,0,2,1:T(8,128)(2,1)} %concatenate.6) | copy-start | bytes 7864324
  61.8 1.7 %copy-start.2 = (f32[8,8]{1,0:T(8,128)S(1)}, f32[8,8]{1,0:T(8,128)}, u32[]{:S(2)}) copy-start(f32[8,8]{1,0:T(8,128)} %constant.24.clone.1) | copy-start | bytes 772
  63.6 1.6 %copy-start.8 = (bf16[1,1,1280,192]{2,3,1,0:T(8,128)(2,1)S(1)}, bf16[1,1,1280,192]{2,3,1,0:T(8,128)(2,1)}, u32[]{:S(2)}) copy-start(bf16[1,1,1280,192]{2,3,1,0:T(8,128)(2,1)} %param.25) | copy-start | bytes 1474564

commit v2 on v1

--- a/solution.py
+++ b/solution.py
@@ -8,20 +8,311 @@
 from jax.sharding import PartitionSpec as P
 
 
-def rectify(inputs, kernel, stride, padding):
-    result = lax.conv_general_dilated(
-        inputs,
-        kernel,
-        (stride, stride),
-        padding,
-        dimension_numbers=("NHWC", "HWIO", "NHWC"),
-        preferred_element_type=jnp.float32,
-    )
-    return jnp.maximum(result, 0.0).astype(jnp.bfloat16)
-
-
-def spatial_mean(inputs):
-    return jnp.mean(inputs.astype(jnp.float32), axis=(1, 2))
+def rectified(lhs, weights):
+    out = jnp.dot(lhs, weights, preferred_element_type=jnp.float32)
+    return jnp.maximum(out, 0.0).astype(jnp.bfloat16)
+
+
+def network_kernel(
+    x_hbm,
+    entry_hbm,
+    wide_hbm,
+    row_hbm,
+    column_hbm,
+    reduce_hbm,
+    second_hbm,
+    second_row_hbm,
+    second_column_hbm,
+    deep_hbm,
+    deep_row_hbm,
+    deep_column_hbm,
+    project_hbm,
+    feats_ref,
+    x_buf,
+    entry_w,
+    wide_w,
+    row_w,
+    column_w,
+    reduce_w,
+    second_w,
+    second_row_w,
+    second_column_w,
+    deep_w,
+    deep_row_w,
+    deep_column_w,
+    project_w,
+    short_buf,
+    long_buf,
+    column_buf,
+    tower_buf,
+    mid_buf,
+    branch_buf,
+    deep_buf,
+    deep_out_buf,
+    average_buf,
+    x_sem,
+    w_sem,
+):
+    grid, _, images, in_ch = x_buf.shape
+    half = row_hbm.shape[1]
+    half_pad = row_w.shape[1]
+    wide = wide_hbm.shape[2]
+    small = mid_buf.shape[0] - 2
+    mid_ch = mid_buf.shape[3]
+    branch = second_row_hbm.shape[1]
+    deep_in = deep_hbm.shape[1]
+    deep_pad = deep_w.shape[1]
+    plain = second_hbm.shape[1] - branch - deep_in
+    margin = (row_hbm.shape[0] - 1) // 2
+
+    for ref in (wide_w, row_w, column_w, reduce_w):
+        ref[:, half:] = jnp.zeros((ref.shape[0], half_pad - half, ref.shape[2]), ref.dtype)
+    deep_w[:, deep_in:] = jnp.zeros(
+        (deep_w.shape[0], deep_pad - deep_in, deep_w.shape[2]), deep_w.dtype
+    )
+
+    def row_copy(h):
+        return pltpu.make_async_copy(x_hbm.at[h], x_buf.at[h], x_sem.at[h])
+
+    pairs = (
+        (entry_hbm, entry_w),
+        (row_hbm, row_w.at[:, 0:half]),
+        (column_hbm, column_w.at[:, 0:half]),
+        (wide_hbm, wide_w.at[:, 0:half]),
+        (reduce_hbm, reduce_w.at[:, 0:half]),
+        (second_hbm, second_w),
+        (second_row_hbm, second_row_w),
+        (second_column_hbm, second_column_w),
+        (deep_hbm, deep_w.at[:, 0:deep_in]),
+        (deep_row_hbm, deep_row_w),
+        (deep_column_hbm, deep_column_w),
+        (project_hbm, project_w),
+    )
+    copies = [
+        pltpu.make_async_copy(source, target, w_sem.at[i])
+        for i, (source, target) in enumerate(pairs)
+    ]
+    copies[0].start()
+    for h in range(grid):
+        row_copy(h).start()
+    for copy in copies[1:]:
+        copy.start()
+
+    low = half // 128 * 128
+    for ref in (short_buf, column_buf, tower_buf):
+        ref[..., low:] = jnp.zeros(ref.shape[:3] + (ref.shape[3] - low,), ref.dtype)
+    long_buf[..., low:] = jnp.zeros(long_buf.shape[:3] + (half_pad - low,), long_buf.dtype)
+    for edge in (pl.ds(0, margin), pl.ds(grid + margin, margin)):
+        long_buf[:, edge] = jnp.zeros((grid, margin, images, half_pad), long_buf.dtype)
+        column_buf[edge] = jnp.zeros((margin, grid, images, half_pad), column_buf.dtype)
+    deep_low = deep_in // 128 * 128
+    deep_buf[..., deep_low:] = jnp.zeros(
+        deep_buf.shape[:3] + (deep_pad - deep_low,), deep_buf.dtype
+    )
+    for ref in (mid_buf, branch_buf, deep_buf, deep_out_buf):
+        line = jnp.zeros((small + 2, images, ref.shape[3]), ref.dtype)
+        ref[0] = line
+        ref[small + 1] = line
+        ref[:, 0] = line
+        ref[:, small + 1] = line
+
+    copies[0].wait()
+
+    def entry_step(h, carry):
+        row_copy(h).wait()
+        out = rectified(x_buf[h].reshape(grid * images, in_ch), entry_w[...])
+        short_buf[h, :, :, 0:half] = out[:, 0:half].reshape(grid, images, half)
+        long_buf[h, pl.ds(margin, grid), :, 0:half] = out[:, half:].reshape(grid, images, half)
+        return carry
+
+    lax.fori_loop(0, grid, entry_step, 0)
+
+    copies[1].wait()
+
+    def row_step(h, carry):
+        lhs = jnp.concatenate(
+            [
+                long_buf[h, pl.ds(j, grid)].reshape(grid * images, half_pad)
+                for j in range(2 * margin + 1)
+            ],
+            axis=1,
+        )
+        out = rectified(lhs, row_w[...].reshape(-1, half))
+        column_buf[h + margin, :, :, 0:half] = out.reshape(grid, images, half)
+        return carry
+
+    lax.fori_loop(0, grid, row_step, 0)
+
+    copies[2].wait()
+
+    def column_step(h, carry):
+        lhs = jnp.concatenate(
+            [
+                column_buf[h + i].reshape(grid * images, half_pad)
+                for i in range(2 * margin + 1)
+            ],
+            axis=1,
+        )
+        out = rectified(lhs, column_w[...].reshape(-1, half))
+        tower_buf[h, :, :, 0:half] = out.reshape(grid, images, half)
+        return carry
+
+    lax.fori_loop(0, grid, column_step, 0)
+
+    group = 4
+    n_groups = small // group
+
+    def strided(ref, r, j):
+        start, odd = j // 2, (j + 1) // 2
+        width = ref.shape[3]
+        return ref[r, pl.ds(start, 2 * small)].reshape(small, 2, images, width)[:, odd]
+
+    def strided_taps(ref, h):
+        return jnp.concatenate(
+            [
+                jnp.concatenate(
+                    [strided(ref, 2 * (h + g) + i, j) for g in range(group)], axis=0
+                ).reshape(group * small * images, half_pad)
+                for i in range(3)
+                for j in range(3)
+            ],
+            axis=1,
+        )
+
+    copies[3].wait()
+    copies[4].wait()
+
+    def middle_step(step, carry):
+        h = step * group
+        wide_out = rectified(strided_taps(short_buf, h), wide_w[...].reshape(-1, wide))
+        tower_out = rectified(strided_taps(tower_buf, h), reduce_w[...].reshape(-1, half))
+        both = jnp.concatenate([wide_out, tower_out], axis=1)
+        mid_buf[pl.ds(h + 1, group), pl.ds(1, small), :, 0 : wide + half] = both.reshape(
+            group, small, images, wide + half
+        )
+        for g in range(group):
+            for lane in range(0, in_ch, 256):
+                lanes = pl.ds(lane, 256)
+                r = 2 * (h + g)
+                tall = jnp.maximum(
+                    jnp.maximum(x_buf[r, :, :, lanes], x_buf[r + 1, :, :, lanes]),
+                    x_buf[r + 2, :, :, lanes],
+                )
+                even = tall[0 : 2 * small].reshape(small, 2, images, 256)
+                late = tall[1 : 2 * small + 1].reshape(small, 2, images, 256)
+                mid_buf[h + g + 1, pl.ds(1, small), :, pl.ds(wide + half + lane, 256)] = (
+                    jnp.maximum(jnp.maximum(even[:, 0], even[:, 1]), late[:, 1])
+                )
+        return carry
+
+    lax.fori_loop(0, n_groups, middle_step, 0)
+
+    rows_m = group * small * images
+    here = pl.ds(1, small)
+
+    def total(out):
+        width = out.shape[1]
+        return jnp.sum(out.astype(jnp.float32).reshape(group * small, images, width), axis=0)
+
+    copies[5].wait()
+
+    def second_step(step, plain_sum):
+        h = step * group
+        lhs = mid_buf[pl.ds(h + 1, group), here].reshape(rows_m, mid_ch)
+        out = rectified(lhs, second_w[...])
+        branch_buf[pl.ds(h + 1, group), here] = out[:, plain : plain + branch].reshape(
+            group, small, images, branch
+        )
+        deep_buf[pl.ds(h + 1, group), here, :, 0:deep_in] = out[:, plain + branch :].reshape(
+            group, small, images, deep_in
+        )
+        return plain_sum + total(out[:, 0:plain])
+
+    plain_sum = lax.fori_loop(
+        0, n_groups, second_step, jnp.zeros((images, plain), jnp.float32)
+    )
+
+    def window(ref, h, rows, cols):
+        return jnp.concatenate(
+            [
+                ref[pl.ds(h + i, group), pl.ds(j, small)].reshape(rows_m, ref.shape[3])
+                for i in rows
+                for j in cols
+            ],
+            axis=1,
+        )
+
+    def pair_step(source, row_weights, column_weights):
+        out_ch = row_weights.shape[2]
+
+        def step_body(step, sums):
+            h = step * group
+            row_out = rectified(
+                window(source, h, (1,), (0, 1, 2)), row_weights[...].reshape(-1, out_ch)
+            )
+            column_out = rectified(
+                window(source, h, (0, 1, 2), (1,)), column_weights[...].reshape(-1, out_ch)
+            )
+            return sums[0] + total(row_out), sums[1] + total(column_out)
+
+        zero = jnp.zeros((images, out_ch), jnp.float32)
+        return lax.fori_loop(0, n_groups, step_body, (zero, zero))
+
+    copies[6].wait()
+    copies[7].wait()
+    row_a, column_a = pair_step(branch_buf, second_row_w, second_column_w)
+
+    copies[8].wait()
+
+    def deep_step(step, carry):
+        h = step * group
+        lhs = window(deep_buf, h, (0, 1, 2), (0, 1, 2))
+        out = rectified(lhs, deep_w[...].reshape(9 * deep_pad, -1))
+        deep_out_buf[pl.ds(h + 1, group), here] = out.reshape(
+            group, small, images, out.shape[1]
+        )
+        return carry
+
+    lax.fori_loop(0, n_groups, deep_step, 0)
+
+    copies[9].wait()
+    copies[10].wait()
+    row_b, column_b = pair_step(deep_out_buf, deep_row_w, deep_column_w)
+
+    def average_step(chunk, carry):
+        lanes = pl.ds(pl.multiple_of(chunk * 128, 128), 128)
+        across = []
+        for r in range(small + 2):
+            line = mid_buf[r, :, :, lanes].astype(jnp.float32)
+            across.append(line[0:small] + line[1 : small + 1] + line[2 : small + 2])
+        for h in range(small):
+            tall = 2 if h in (0, small - 1) else 3
+            summed = across[h] + across[h + 1] + across[h + 2]
+            average_buf[h, 0, :, lanes] = (summed[0] * (1.0 / (2 * tall))).astype(jnp.bfloat16)
+            average_buf[h, pl.ds(1, small - 2), :, lanes] = (
+                summed[1 : small - 1] * (1.0 / (3 * tall))
+            ).astype(jnp.bfloat16)
+            average_buf[h, small - 1, :, lanes] = (
+                summed[small - 1] * (1.0 / (2 * tall))
+            ).astype(jnp.bfloat16)
+        return carry
+
+    lax.fori_loop(0, mid_ch // 128, average_step, 0)
+
+    copies[11].wait()
+
+    def project_step(step, pooled_sum):
+        lhs = average_buf[pl.ds(step * group, group)].reshape(rows_m, mid_ch)
+        out = lax.dot_general(
+            lhs, project_w[...], (((1,), (1,)), ((), ())), preferred_element_type=jnp.float32
+        )
+        return pooled_sum + total(jnp.maximum(out, 0.0).astype(jnp.bfloat16))
+
+    pooled = lax.fori_loop(
+        0, n_groups, project_step, jnp.zeros((images, project_w.shape[0]), jnp.float32)
+    )
+    features = jnp.concatenate([plain_sum, row_a, column_a, row_b, column_b, pooled], axis=1)
+    feats_ref[...] = features * (1.0 / (small * small))
 
 
 def network(
@@ -39,60 +330,79 @@
     deep_column,
     pool_project,
 ):
-    no_margin = ((0, 0), (0, 0))
-    entry_out = rectify(block_inputs, first_entry, 1, no_margin)
-    half_width = first_wide.shape[2]
-    wide_out = rectify(entry_out[..., :half_width], first_wide, 2, no_margin)
-    tower_out = rectify(entry_out[..., half_width:], first_row, 1, ((0, 0), (3, 3)))
-    tower_out = rectify(tower_out, first_column, 1, ((3, 3), (0, 0)))
-    tower_out = rectify(tower_out, first_reduce, 2, no_margin)
-    maximum = lax.reduce_window(
-        block_inputs,
-        jnp.array(-jnp.inf, block_inputs.dtype),
-        lax.max,
-        (1, 3, 3, 1),
-        (1, 2, 2, 1),
-        "VALID",
-    )
-    middle = jnp.concatenate([wide_out, tower_out, maximum], axis=3)
-    second = rectify(middle, second_entry, 1, no_margin)
-    branch_width = second_row.shape[2]
-    deep_width = second_deep.shape[2]
-    plain_width = second_entry.shape[3] - branch_width - deep_width
-    plain_out = second[..., :plain_width]
-    branch_in = second[..., plain_width : plain_width + branch_width]
-    deep_in = second[..., plain_width + branch_width :]
-    row_a = rectify(branch_in, second_row, 1, ((0, 0), (1, 1)))
-    col_a = rectify(branch_in, second_column, 1, ((1, 1), (0, 0)))
-    deep_out = rectify(deep_in, second_deep, 1, ((1, 1), (1, 1)))
-    row_b = rectify(deep_out, deep_row, 1, ((0, 0), (1, 1)))
-    col_b = rectify(deep_out, deep_column, 1, ((1, 1), (0, 0)))
-    pool_pad = ((0, 0), (1, 1), (1, 1), (0, 0))
-    summed = lax.reduce_window(
-        middle.astype(jnp.float32),
-        jnp.array(0.0, jnp.float32),
-        lax.add,
-        (1, 3, 3, 1),
-        (1, 1, 1, 1),
-        pool_pad,
-    )
-    ones_map = jnp.ones((1, middle.shape[1], middle.shape[2], 1), jnp.float32)
-    cell_count = lax.reduce_window(
-        ones_map, jnp.array(0.0, jnp.float32), lax.add, (1, 3, 3, 1), (1, 1, 1, 1), pool_pad
-    )
-    averaged = (summed / cell_count).astype(jnp.bfloat16)
-    pooled = rectify(averaged, pool_project, 1, no_margin)
-    return jnp.concatenate(
-        [
-            spatial_mean(plain_out),
-            spatial_mean(row_a),
-            spatial_mean(col_a),
-            spatial_mean(row_b),
-            spatial_mean(col_b),
-            spatial_mean(pooled),
+    def flat(kernel):
+        return kernel.reshape((-1,) + kernel.shape[2:])
+
+    x = jnp.transpose(block_inputs, (1, 2, 0, 3))
+    grid, _, images, in_ch = x.shape
+    small = (grid - 3) // 2 + 1
+    half = first_row.shape[2]
+    half_pad = -(-half // 256) * 256
+    deep_in = second_deep.shape[2]
+    deep_pad = -(-deep_in // 128) * 128
+    margin = (first_row.shape[1] - 1) // 2
+    mid_ch = second_entry.shape[2]
+    branch = second_row.shape[2]
+    deep_ch = second_deep.shape[3]
+    operands = [
+        x,
+        first_entry[0, 0],
+        flat(first_wide),
+        flat(first_row),
+        flat(first_column),
+        flat(first_reduce),
+        second_entry[0, 0],
+        flat(second_row),
+        flat(second_column),
+        flat(second_deep),
+        flat(deep_row),
+        flat(deep_column),
+        pool_project[0, 0].T,
+    ]
+    width = second_entry.shape[3] - branch - deep_in + 2 * branch + 2 * deep_ch
+    width += pool_project.shape[3]
+
+    def scratch(*shape):
+        return pltpu.VMEM(shape, jnp.bfloat16)
+
+    def weight_scratch(kernel, depth):
+        return scratch(kernel.shape[0], depth, kernel.shape[2])
+
+    edge = small + 2
+    return pl.pallas_call(
+        network_kernel,
+        out_shape=jax.ShapeDtypeStruct((images, width), jnp.float32),
+        in_specs=[pl.BlockSpec(memory_space=pl.ANY)] * len(operands),
+        out_specs=pl.BlockSpec(memory_space=pltpu.VMEM),
+        scratch_shapes=[
+            scratch(*x.shape),
+            scratch(*operands[1].shape),
+            weight_scratch(operands[2], half_pad),
+            weight_scratch(operands[3], half_pad),
+            weight_scratch(operands[4], half_pad),
+            weight_scratch(operands[5], half_pad),
+            scratch(*operands[6].shape),
+            scratch(*operands[7].shape),
+            scratch(*operands[8].shape),
+            weight_scratch(operands[9], deep_pad),
+            scratch(*operands[10].shape),
+            scratch(*operands[11].shape),
+            scratch(*operands[12].shape),
+            scratch(grid, grid, images, half_pad),
+            scratch(grid, grid + 2 * margin, images, half_pad),
+            scratch(grid + 2 * margin, grid, images, half_pad),
+            scratch(grid, grid, images, half_pad),
+            scratch(edge, edge, images, mid_ch),
+            scratch(edge, edge, images, branch),
+            scratch(edge, edge, images, deep_pad),
+            scratch(edge, edge, images, deep_ch),
+            scratch(small, small, images, mid_ch),
+            pltpu.SemaphoreType.DMA((grid,)),
+            pltpu.SemaphoreType.DMA((len(operands) - 1,)),
         ],
-        axis=1,
-    )
+        compiler_params=pltpu.CompilerParams(vmem_limit_bytes=60 * 1024 * 1024),
+        name="network",
+    )(*operands)
 
 
 def exchange_kernel(

time: 92.6 us -> 76.3 us (0.82)
  matrix products: 50.8 us -> 0 us
  Pallas kernels: 24.7 us -> 73.2 us
  other arithmetic: 7.28 us -> 0 us
  local copies, waits for them, and re-layouts: 8.69 us -> 2.29 us
    conv_general_dilated x11 -> x0, matrix products: 50.8 us -> none  [rectify(): lax.conv_general_dilated(inputs, kernel, (stride, stride), padding, dimen...]
    pallas_call x0 -> x1, Pallas kernels: none -> 48.5 us  [network(): pl.pallas_call(network_kernel, out_shape=jax.ShapeDtypeStruct((images, wi...]
    another operation x2 -> x0, other arithmetic: 7.09 us -> none  [the longest x1 5.53 us: network(): lax.reduce_window(block_inputs, jnp.array(-jnp.inf, block_inputs.dtype),...]
    concatenate x2 -> x0, local copies, waits for them, and re-layouts: 5.49 us -> none  [the longest x1 5.38 us: network(): middle = jnp.concatenate([wide_out, tower_out, maximum], axis=3)]
    unnamed x22 -> x4, local copies, waits for them, and re-layouts: 3.2 us -> 2.29 us
where the time goes in v2:
time: 76.3 us; the launch traced here: 76.2 us
  Pallas kernels  73.2 us (96%)
  local copies, waits for them, and re-layouts  2.29 us (3%)
    pallas_call x1, Pallas kernels, network(): pl.pallas_call(network_kernel, out_shape=jax.ShapeDtypeStruct((images, wi...  48.5 us
    pallas_call x1, Pallas kernels, exchange(): pl.pallas_call(functools.partial(exchange_kernel, n_sample, n_col), out_s...  24.7 us
    unnamed x4, local copies, waits for them, and re-layouts  2.29 us

profile of v2, /device:TPU:0, one launch (start us, length us, event | category | flops | bytes accessed | tf_op | source)
XLA Modules:
  0.0 76.2 jit_solution(5244943678518032105)
XLA Ops:
  0.6 48.5 %network.1.feats_ref = f32[16,2048]{1,0:T(8,128)} custom-call(bf16[17,17,16,768]{3,2,1,0:T(8,128)(2,1)} %bitcast.17, bf16[768,384]{1,0:T(8,128)(2,1)} %bitcast.28, bf16[9,192,320]{2,1,0:T(8,128)(2,1)} %bitcast.20, bf16[7,192,192]{2,1,0:T(8,128)(2,1)} %bitcast.26, bf16[7,192,192]{2,1,0:T(8,128)(2,1)} %bitcast.27, bf16[9,192,192]{2,1,0:T(8,128)(2,1)} %bitcast.21, ...), custom_call_target="tpu_custom_call" | custom-call | tf_op jit(solution)/shard_map/network/pallas_call | solution.py:372
  49.2 0.0 copy-start
  49.2 0.9 %copy-done = f32[16,2048]{1,0:T(8,128)S(1)} copy-done((f32[16,2048]{1,0:T(8,128)S(1)}, f32[16,2048]{1,0:T(8,128)}, u32[]{:S(2)}) %copy-start) | copy-done | bytes 131096
  50.1 24.7 %exchange.1 = (f32[1,2048]{1,0:T(1,128)S(1)}, f32[256,512]{1,0:T(8,128)S(1)}) custom-call(f32[16,2048]{1,0:T(8,128)S(1)} %copy-done), custom_call_target="tpu_custom_call" | custom-call | tf_op jit(solution)/shard_map/exchange/pallas_call | solution.py:541
  74.8 0.6 copy.17
  75.4 0.8 %copy.18 = f32[256,512]{1,0:T(8,128)} copy(f32[256,512]{1,0:T(8,128)S(1)} %get-tuple-element.9) | data formatting | bytes 1048576
Async XLA Ops:
  49.2 0.9 %copy-start = (f32[16,2048]{1,0:T(8,128)S(1)}, f32[16,2048]{1,0:T(8,128)}, u32[]{:S(2)}) copy-start(f32[16,2048]{1,0:T(8,128)} %network.1.feats_ref) | copy-start | bytes 393220

commit v3 on v2

--- a/solution.py
+++ b/solution.py
@@ -65,12 +65,6 @@
     plain = second_hbm.shape[1] - branch - deep_in
     margin = (row_hbm.shape[0] - 1) // 2
 
-    for ref in (wide_w, row_w, column_w, reduce_w):
-        ref[:, half:] = jnp.zeros((ref.shape[0], half_pad - half, ref.shape[2]), ref.dtype)
-    deep_w[:, deep_in:] = jnp.zeros(
-        (deep_w.shape[0], deep_pad - deep_in, deep_w.shape[2]), deep_w.dtype
-    )
-
     def row_copy(h):
         return pltpu.make_async_copy(x_hbm.at[h], x_buf.at[h], x_sem.at[h])
 
@@ -95,6 +89,11 @@
     copies[0].start()
     for h in range(grid):
         row_copy(h).start()
+    for ref in (wide_w, row_w, column_w, reduce_w):
+        ref[:, half:] = jnp.zeros((ref.shape[0], half_pad - half, ref.shape[2]), ref.dtype)
+    deep_w[:, deep_in:] = jnp.zeros(
+        (deep_w.shape[0], deep_pad - deep_in, deep_w.shape[2]), deep_w.dtype
+    )
     for copy in copies[1:]:
         copy.start()
 
@@ -118,48 +117,59 @@
 
     copies[0].wait()
 
-    def entry_step(h, carry):
-        row_copy(h).wait()
-        out = rectified(x_buf[h].reshape(grid * images, in_ch), entry_w[...])
-        short_buf[h, :, :, 0:half] = out[:, 0:half].reshape(grid, images, half)
-        long_buf[h, pl.ds(margin, grid), :, 0:half] = out[:, half:].reshape(grid, images, half)
-        return carry
-
-    lax.fori_loop(0, grid, entry_step, 0)
+    tall = 4
+
+    def by_rows(step_body):
+        def looped(step, carry):
+            step_body(step * tall, tall)
+            return carry
+
+        lax.fori_loop(0, grid // tall, looped, 0)
+        if grid % tall:
+            step_body(grid // tall * tall, grid % tall)
+
+    def entry_step(h, n):
+        for g in range(n):
+            row_copy(h + g).wait()
+        out = rectified(x_buf[pl.ds(h, n)].reshape(n * grid * images, in_ch), entry_w[...])
+        short_buf[pl.ds(h, n), :, :, 0:half] = out[:, 0:half].reshape(n, grid, images, half)
+        long_buf[pl.ds(h, n), pl.ds(margin, grid), :, 0:half] = out[:, half:].reshape(
+            n, grid, images, half
+        )
+
+    by_rows(entry_step)
 
     copies[1].wait()
 
-    def row_step(h, carry):
+    def row_step(h, n):
         lhs = jnp.concatenate(
             [
-                long_buf[h, pl.ds(j, grid)].reshape(grid * images, half_pad)
+                long_buf[pl.ds(h, n), pl.ds(j, grid)].reshape(n * grid * images, half_pad)
                 for j in range(2 * margin + 1)
             ],
             axis=1,
         )
         out = rectified(lhs, row_w[...].reshape(-1, half))
-        column_buf[h + margin, :, :, 0:half] = out.reshape(grid, images, half)
-        return carry
-
-    lax.fori_loop(0, grid, row_step, 0)
+        column_buf[pl.ds(h + margin, n), :, :, 0:half] = out.reshape(n, grid, images, half)
+
+    by_rows(row_step)
 
     copies[2].wait()
 
-    def column_step(h, carry):
+    def column_step(h, n):
         lhs = jnp.concatenate(
             [
-                column_buf[h + i].reshape(grid * images, half_pad)
+                column_buf[pl.ds(h + i, n)].reshape(n * grid * images, half_pad)
                 for i in range(2 * margin + 1)
             ],
             axis=1,
         )
         out = rectified(lhs, column_w[...].reshape(-1, half))
-        tower_buf[h, :, :, 0:half] = out.reshape(grid, images, half)
-        return carry
-
-    lax.fori_loop(0, grid, column_step, 0)
-
-    group = 4
+        tower_buf[pl.ds(h, n), :, :, 0:half] = out.reshape(n, grid, images, half)
+
+    by_rows(column_step)
+
+    group = small
     n_groups = small // group
 
     def strided(ref, r, j):
@@ -194,12 +204,12 @@
             for lane in range(0, in_ch, 256):
                 lanes = pl.ds(lane, 256)
                 r = 2 * (h + g)
-                tall = jnp.maximum(
+                lines = jnp.maximum(
                     jnp.maximum(x_buf[r, :, :, lanes], x_buf[r + 1, :, :, lanes]),
                     x_buf[r + 2, :, :, lanes],
                 )
-                even = tall[0 : 2 * small].reshape(small, 2, images, 256)
-                late = tall[1 : 2 * small + 1].reshape(small, 2, images, 256)
+                even = lines[0 : 2 * small].reshape(small, 2, images, 256)
+                late = lines[1 : 2 * small + 1].reshape(small, 2, images, 256)
                 mid_buf[h + g + 1, pl.ds(1, small), :, pl.ds(wide + half + lane, 256)] = (
                     jnp.maximum(jnp.maximum(even[:, 0], even[:, 1]), late[:, 1])
                 )
@@ -286,14 +296,14 @@
             line = mid_buf[r, :, :, lanes].astype(jnp.float32)
             across.append(line[0:small] + line[1 : small + 1] + line[2 : small + 2])
         for h in range(small):
-            tall = 2 if h in (0, small - 1) else 3
+            high = 2 if h in (0, small - 1) else 3
             summed = across[h] + across[h + 1] + across[h + 2]
-            average_buf[h, 0, :, lanes] = (summed[0] * (1.0 / (2 * tall))).astype(jnp.bfloat16)
+            average_buf[h, 0, :, lanes] = (summed[0] * (1.0 / (2 * high))).astype(jnp.bfloat16)
             average_buf[h, pl.ds(1, small - 2), :, lanes] = (
-                summed[1 : small - 1] * (1.0 / (3 * tall))
+                summed[1 : small - 1] * (1.0 / (3 * high))
             ).astype(jnp.bfloat16)
             average_buf[h, small - 1, :, lanes] = (
-                summed[small - 1] * (1.0 / (2 * tall))
+                summed[small - 1] * (1.0 / (2 * high))
             ).astype(jnp.bfloat16)
         return carry
 

time: 76.3 us -> 72.3 us (0.948)
  Pallas kernels: 73.2 us -> 69.2 us
    pallas_call x1, Pallas kernels: 48.5 us -> 44.5 us  [network(): pl.pallas_call(network_kernel, out_shape=jax.ShapeDtypeStruct((images, wi...]
where the time goes in v3:
time: 72.3 us; the launch traced here: 72.1 us
  Pallas kernels  69.2 us (96%)
  local copies, waits for them, and re-layouts  2.29 us (3%)
    pallas_call x1, Pallas kernels, network(): pl.pallas_call(network_kernel, out_shape=jax.ShapeDtypeStruct((images, wi...  44.5 us
    pallas_call x1, Pallas kernels, exchange(): pl.pallas_call(functools.partial(exchange_kernel, n_sample, n_col), out_s...  24.7 us
    unnamed x4, local copies, waits for them, and re-layouts  2.29 us

profile of v3, /device:TPU:0, one launch (start us, length us, event | category | flops | bytes accessed | tf_op | source)
XLA Modules:
  0.0 72.1 jit_solution(11666981464897187962)
XLA Ops:
  0.6 44.5 %network.1.feats_ref = f32[16,2048]{1,0:T(8,128)} custom-call(bf16[17,17,16,768]{3,2,1,0:T(8,128)(2,1)} %bitcast.17, bf16[768,384]{1,0:T(8,128)(2,1)} %bitcast.28, bf16[9,192,320]{2,1,0:T(8,128)(2,1)} %bitcast.20, bf16[7,192,192]{2,1,0:T(8,128)(2,1)} %bitcast.26, bf16[7,192,192]{2,1,0:T(8,128)(2,1)} %bitcast.27, bf16[9,192,192]{2,1,0:T(8,128)(2,1)} %bitcast.21, ...), custom_call_target="tpu_custom_call" | custom-call | tf_op jit(solution)/shard_map/network/pallas_call | solution.py:382
  45.1 0.0 copy-start
  45.1 0.9 %copy-done = f32[16,2048]{1,0:T(8,128)S(1)} copy-done((f32[16,2048]{1,0:T(8,128)S(1)}, f32[16,2048]{1,0:T(8,128)}, u32[]{:S(2)}) %copy-start) | copy-done | bytes 131096
  46.0 24.7 %exchange.1 = (f32[1,2048]{1,0:T(1,128)S(1)}, f32[256,512]{1,0:T(8,128)S(1)}) custom-call(f32[16,2048]{1,0:T(8,128)S(1)} %copy-done), custom_call_target="tpu_custom_call" | custom-call | tf_op jit(solution)/shard_map/exchange/pallas_call | solution.py:551
  70.7 0.6 copy.17
  71.3 0.8 %copy.18 = f32[256,512]{1,0:T(8,128)} copy(f32[256,512]{1,0:T(8,128)S(1)} %get-tuple-element.9) | data formatting | bytes 1048576
Async XLA Ops:
  45.1 0.9 %copy-start = (f32[16,2048]{1,0:T(8,128)S(1)}, f32[16,2048]{1,0:T(8,128)}, u32[]{:S(2)}) copy-start(f32[16,2048]{1,0:T(8,128)} %network.1.feats_ref) | copy-start | bytes 393220

commit v4 on v3

--- a/solution.py
+++ b/solution.py
@@ -6,6 +6,12 @@
 from jax.experimental import pallas as pl
 from jax.experimental.pallas import tpu as pltpu
 from jax.sharding import PartitionSpec as P
+
+
+def in_turn(steps, step_body, carry):
+    for step in range(steps):
+        carry = step_body(step, carry)
+    return carry
 
 
 def rectified(lhs, weights):
@@ -189,8 +195,8 @@
             axis=1,
         )
 
-    copies[3].wait()
-    copies[4].wait()
+    for copy in copies[3:]:
+        copy.wait()
 
     def middle_step(step, carry):
         h = step * group
@@ -215,7 +221,7 @@
                 )
         return carry
 
-    lax.fori_loop(0, n_groups, middle_step, 0)
+    in_turn(n_groups, middle_step, 0)
 
     rows_m = group * small * images
     here = pl.ds(1, small)
@@ -223,8 +229,6 @@
     def total(out):
         width = out.shape[1]
         return jnp.sum(out.astype(jnp.float32).reshape(group * small, images, width), axis=0)
-
-    copies[5].wait()
 
     def second_step(step, plain_sum):
         h = step * group
@@ -238,8 +242,8 @@
         )
         return plain_sum + total(out[:, 0:plain])
 
-    plain_sum = lax.fori_loop(
-        0, n_groups, second_step, jnp.zeros((images, plain), jnp.float32)
+    plain_sum = in_turn(
+        n_groups, second_step, jnp.zeros((images, plain), jnp.float32)
     )
 
     def window(ref, h, rows, cols):
@@ -266,13 +270,9 @@
             return sums[0] + total(row_out), sums[1] + total(column_out)
 
         zero = jnp.zeros((images, out_ch), jnp.float32)
-        return lax.fori_loop(0, n_groups, step_body, (zero, zero))
-
-    copies[6].wait()
-    copies[7].wait()
+        return in_turn(n_groups, step_body, (zero, zero))
+
     row_a, column_a = pair_step(branch_buf, second_row_w, second_column_w)
-
-    copies[8].wait()
 
     def deep_step(step, carry):
         h = step * group
@@ -283,14 +283,12 @@
         )
         return carry
 
-    lax.fori_loop(0, n_groups, deep_step, 0)
-
-    copies[9].wait()
-    copies[10].wait()
+    in_turn(n_groups, deep_step, 0)
+
     row_b, column_b = pair_step(deep_out_buf, deep_row_w, deep_column_w)
 
     def average_step(chunk, carry):
-        lanes = pl.ds(pl.multiple_of(chunk * 128, 128), 128)
+        lanes = pl.ds(chunk * 128, 128)
         across = []
         for r in range(small + 2):
             line = mid_buf[r, :, :, lanes].astype(jnp.float32)
@@ -307,9 +305,7 @@
             ).astype(jnp.bfloat16)
         return carry
 
-    lax.fori_loop(0, mid_ch // 128, average_step, 0)
-
-    copies[11].wait()
+    in_turn(mid_ch // 128, average_step, 0)
 
     def project_step(step, pooled_sum):
         lhs = average_buf[pl.ds(step * group, group)].reshape(rows_m, mid_ch)
@@ -318,8 +314,8 @@
         )
         return pooled_sum + total(jnp.maximum(out, 0.0).astype(jnp.bfloat16))
 
-    pooled = lax.fori_loop(
-        0, n_groups, project_step, jnp.zeros((images, project_w.shape[0]), jnp.float32)
+    pooled = in_turn(
+        n_groups, project_step, jnp.zeros((images, project_w.shape[0]), jnp.float32)
     )
     features = jnp.concatenate([plain_sum, row_a, column_a, row_b, column_b, pooled], axis=1)
     feats_ref[...] = features * (1.0 / (small * small))
@@ -418,9 +414,12 @@
 def exchange_kernel(
     n_sample,
     n_col,
-    feats_ref,
+    feats_hbm,
     mean_ref,
     cov_ref,
+    feats_ref,
+    cols_high,
+    cols_low,
     cols,
     rows,
     sums_col,
@@ -437,6 +436,9 @@
     rows_recv,
     total_send,
     total_recv,
+    pair_send,
+    pair_recv,
+    fetch_sem,
 ):
     s = lax.axis_index("sample")
     c = lax.axis_index("col")
@@ -464,6 +466,8 @@
         copy.start()
         return copy
 
+    fetch = pltpu.make_async_copy(feats_hbm, feats_ref, fetch_sem)
+    fetch.start()
     barrier = pltpu.get_barrier_semaphore()
     for k in range(1, n_col):
         pl.semaphore_signal(
@@ -473,42 +477,78 @@
         pl.semaphore_signal(
             barrier, inc=1, device_id=(lax.rem(s + k, n_sample), c), device_id_type=mesh_id
         )
+    fetch.wait()
     sums_col[c] = jnp.sum(feats_ref[...], axis=0, keepdims=True)
     cols[s, c] = feats_ref[:, col_at(c)]
     rows[s, c] = feats_ref[:, row_at(s)]
     pl.semaphore_wait(barrier, n_col - 1 + n_sample - 1)
 
-    sends = []
     first_cols, first_sums, first_rows = [], [], []
     for k in range(1, n_col):
         to = lax.rem(c + k, n_col)
+        first_sums.append(
+            send(sums_col.at[c], sums_col.at[c], sum_send.at[k], sum_recv.at[k], s, to)
+        )
         first_cols.append(
             send(feats_ref.at[:, col_at(to)], cols.at[s, c], col_send.at[k], col_recv.at[k], s, to)
-        )
-        first_sums.append(
-            send(sums_col.at[c], sums_col.at[c], sum_send.at[k], sum_recv.at[k], s, to)
         )
     for k in range(1, n_sample):
         to = lax.rem(s + k, n_sample)
         first_rows.append(
             send(feats_ref.at[:, row_at(to)], rows.at[s, c], row_send.at[k], row_recv.at[k], to, c)
         )
-    for copy in first_rows:
-        copy.wait_recv()
-    second_rows = []
-    for k in range(1, n_col):
-        to = lax.rem(c + k, n_col)
-        second_rows.append(
-            send(rows.at[:, c], rows.at[:, c], rows_send.at[k], rows_recv.at[k], s, to)
-        )
-    for copy in first_cols:
-        copy.wait_recv()
-    second_cols = []
-    for k in range(1, n_sample):
-        to = lax.rem(s + k, n_sample)
-        second_cols.append(
-            send(cols.at[s], cols.at[s], cols_send.at[k], cols_recv.at[k], to, c)
-        )
+
+    pair = 2 if n_sample % 2 == 0 else 1
+    n_pairs = n_sample // pair
+    mine = lax.rem(s, pair)
+    sibling = s + 1 - 2 * mine
+
+    def same_side(k):
+        return lax.rem(s // pair + k + n_pairs, n_pairs) * pair + mine
+
+    def hand_on(slot, k):
+        return send(cols.at[slot], cols.at[slot], pair_send.at[k], pair_recv.at[k], sibling, c)
+
+    def hop(plane, to, index):
+        return pltpu.make_async_remote_copy(
+            src_ref=rows.at[:, plane],
+            dst_ref=rows.at[:, plane],
+            send_sem=rows_send.at[index],
+            recv_sem=rows_recv.at[index],
+            device_id=(s, to),
+            device_id_type=mesh_id,
+        )
+
+    def send_right(k):
+        return (c + 1 < n_col) & (c >= k - 1)
+
+    def send_left(k):
+        return (c >= 1) & (c + k - 1 < n_col)
+
+    def right(k):
+        return hop(lax.rem(c - k + 1 + n_col, n_col), lax.rem(c + 1, n_col), k)
+
+    def left(k):
+        return hop(lax.rem(c + k - 1, n_col), lax.rem(c - 1 + n_col, n_col), n_col + k)
+
+    def start_hops(k):
+        @pl.when(send_right(k))
+        def _():
+            right(k).start()
+
+        @pl.when(send_left(k))
+        def _():
+            left(k).start()
+
+    def finish_hops(k):
+        @pl.when(c >= k)
+        def _():
+            right(k).wait_recv()
+
+        @pl.when(c + k < n_col)
+        def _():
+            left(k).wait_recv()
+
     for copy in first_sums:
         copy.wait_recv()
     sums_sample[s] = jnp.sum(sums_col[...], axis=0)
@@ -518,26 +558,63 @@
         second_sums.append(
             send(sums_sample.at[s], sums_sample.at[s], total_send.at[k], total_recv.at[k], to, c)
         )
+    for copy in first_rows:
+        copy.wait_recv()
+    start_hops(1)
+    for copy in first_cols:
+        copy.wait_recv()
+    second_cols = []
+    for k in range(1, n_pairs):
+        second_cols.append(
+            send(cols.at[s], cols.at[s], cols_send.at[k], cols_recv.at[k], same_side(k), c)
+        )
+    handed = [hand_on(s, 0)] if pair == 2 else []
     for copy in second_sums:
         copy.wait_recv()
     mean_ref[...] = jnp.sum(sums_sample[...], axis=0) * (1.0 / total_images)
-    for copy in second_rows:
+
+    def prepare(slot):
+        values = cols[slot].reshape(n_col * images, col_width) - mean_ref[:, col_at(c)]
+        high = values.astype(jnp.bfloat16)
+        cols_high[slot] = high
+        cols_low[slot] = (values - high.astype(jnp.float32)).astype(jnp.bfloat16)
+
+    prepare(s)
+    for k in range(1, max(n_col, n_pairs)):
+        if k < n_pairs:
+            second_cols[k - 1].wait_recv()
+            if pair == 2:
+                handed.append(hand_on(same_side(-k), k))
+        if k < n_col:
+            finish_hops(k)
+            if k + 1 < n_col:
+                start_hops(k + 1)
+        if k < n_pairs:
+            prepare(same_side(-k))
+    for k, copy in enumerate(handed):
         copy.wait_recv()
+        prepare(same_side(-k) + 1 - 2 * mine)
     row_values = rows[...].reshape(total_images, row_width) - mean_ref[:, row_at(s)]
     row_values = row_values.T
     row_high = row_values.astype(jnp.bfloat16)
     row_low = (row_values - row_high.astype(jnp.float32)).astype(jnp.bfloat16)
-    for copy in second_cols:
-        copy.wait_recv()
-    col_values = cols[...].reshape(total_images, col_width) - mean_ref[:, col_at(c)]
-    col_high = col_values.astype(jnp.bfloat16)
-    col_low = (col_values - col_high.astype(jnp.float32)).astype(jnp.bfloat16)
+    col_high = cols_high[...].reshape(total_images, col_width)
+    col_low = cols_low[...].reshape(total_images, col_width)
     product = jnp.dot(row_high, col_low, preferred_element_type=jnp.float32)
     product += jnp.dot(row_low, col_high, preferred_element_type=jnp.float32)
     product += jnp.dot(row_high, col_high, preferred_element_type=jnp.float32)
     cov_ref[...] = product * (1.0 / (total_images - 1))
-    for copy in first_cols + first_sums + first_rows + second_rows + second_cols + second_sums:
+    for copy in first_cols + first_sums + first_rows + second_cols + second_sums + handed:
         copy.wait_send()
+    for k in range(1, n_col):
+
+        @pl.when(send_right(k))
+        def _():
+            right(k).wait_send()
+
+        @pl.when(send_left(k))
+        def _():
+            left(k).wait_send()
 
 
 def exchange(features):
@@ -554,9 +631,12 @@
             jax.ShapeDtypeStruct((1, width), jnp.float32),
             jax.ShapeDtypeStruct((row_width, col_width), jnp.float32),
         ),
-        in_specs=[vmem],
+        in_specs=[pl.BlockSpec(memory_space=pl.ANY)],
         out_specs=(vmem, vmem),
         scratch_shapes=[
+            pltpu.VMEM((images, width), jnp.float32),
+            pltpu.VMEM((n_sample, n_col * images, col_width), jnp.bfloat16),
+            pltpu.VMEM((n_sample, n_col * images, col_width), jnp.bfloat16),
             pltpu.VMEM((n_sample, n_col, images, col_width), jnp.float32),
             pltpu.VMEM((n_sample, n_col, images, row_width), jnp.float32),
             pltpu.VMEM((n_col, 1, width), jnp.float32),
@@ -569,10 +649,13 @@
             dma((n_col,)),
             dma((n_sample,)),
             dma((n_sample,)),
-            dma((n_col,)),
-            dma((n_col,)),
+            dma((2 * n_col,)),
+            dma((2 * n_col,)),
             dma((n_sample,)),
             dma((n_sample,)),
+            dma((n_sample,)),
+            dma((n_sample,)),
+            dma,
         ],
         compiler_params=pltpu.CompilerParams(
             collective_id=0, has_side_effects=True, vmem_limit_bytes=48 * 1024 * 1024

time: 72.3 us -> 70.2 us (0.971)
  Pallas kernels: 69.2 us -> 67.2 us
    pallas_call x1, Pallas kernels: 44.5 us -> 41.5 us  [network(): pl.pallas_call(network_kernel, out_shape=jax.ShapeDtypeStruct((images, wi...]
    pallas_call x1, Pallas kernels: 24.7 us -> 25.6 us  [exchange(): pl.pallas_call(functools.partial(exchange_kernel, n_sample, n_col), out_s...]
where the time goes in v4:
time: 70.2 us; the launch traced here: 70.1 us
  Pallas kernels  67.2 us (96%)
  local copies, waits for them, and re-layouts  2.29 us (3%)
    pallas_call x1, Pallas kernels, network(): pl.pallas_call(network_kernel, out_shape=jax.ShapeDtypeStruct((images, wi...  41.5 us
    pallas_call x1, Pallas kernels, exchange(): pl.pallas_call(functools.partial(exchange_kernel, n_sample, n_col), out_s...  25.6 us
    unnamed x4, local copies, waits for them, and re-layouts  2.29 us

profile of v4, /device:TPU:0, one launch (start us, length us, event | category | flops | bytes accessed | tf_op | source)
XLA Modules:
  0.0 70.1 jit_solution(3083981834613925485)
XLA Ops:
  0.6 41.5 %network.1.feats_hbm = f32[16,2048]{1,0:T(8,128)} custom-call(bf16[17,17,16,768]{3,2,1,0:T(8,128)(2,1)} %bitcast.17, bf16[768,384]{1,0:T(8,128)(2,1)} %bitcast.28, bf16[9,192,320]{2,1,0:T(8,128)(2,1)} %bitcast.20, bf16[7,192,192]{2,1,0:T(8,128)(2,1)} %bitcast.26, bf16[7,192,192]{2,1,0:T(8,128)(2,1)} %bitcast.27, bf16[9,192,192]{2,1,0:T(8,128)(2,1)} %bitcast.21, ...), custom_call_target="tpu_custom_call" | custom-call | tf_op jit(solution)/shard_map/network/pallas_call | solution.py:378
  42.2 0.0 copy-start
  42.2 0.9 %copy-done = f32[16,2048]{1,0:T(8,128)S(1)} copy-done((f32[16,2048]{1,0:T(8,128)S(1)}, f32[16,2048]{1,0:T(8,128)}, u32[]{:S(2)}) %copy-start) | copy-done | bytes 131096
  43.1 25.6 %exchange.1 = (f32[1,2048]{1,0:T(1,128)S(1)}, f32[256,512]{1,0:T(8,128)S(1)}) custom-call(f32[16,2048]{1,0:T(8,128)S(1)} %copy-done), custom_call_target="tpu_custom_call" | custom-call | tf_op jit(solution)/shard_map/exchange/pallas_call | solution.py:628
  68.7 0.6 copy.17
  69.3 0.8 %copy.18 = f32[256,512]{1,0:T(8,128)} copy(f32[256,512]{1,0:T(8,128)S(1)} %get-tuple-element.9) | data formatting | bytes 1048576
Async XLA Ops:
  42.2 0.9 %copy-start = (f32[16,2048]{1,0:T(8,128)S(1)}, f32[16,2048]{1,0:T(8,128)}, u32[]{:S(2)}) copy-start(f32[16,2048]{1,0:T(8,128)} %network.1.feats_hbm) | copy-start | bytes 393220

commit v5 on v4

--- a/solution.py
+++ b/solution.py
@@ -123,9 +123,7 @@
 
     copies[0].wait()
 
-    tall = 4
-
-    def by_rows(step_body):
+    def by_rows(step_body, tall):
         def looped(step, carry):
             step_body(step * tall, tall)
             return carry
@@ -143,7 +141,7 @@
             n, grid, images, half
         )
 
-    by_rows(entry_step)
+    by_rows(entry_step, 4)
 
     copies[1].wait()
 
@@ -158,7 +156,7 @@
         out = rectified(lhs, row_w[...].reshape(-1, half))
         column_buf[pl.ds(h + margin, n), :, :, 0:half] = out.reshape(n, grid, images, half)
 
-    by_rows(row_step)
+    by_rows(row_step, 8)
 
     copies[2].wait()
 
@@ -173,7 +171,7 @@
         out = rectified(lhs, column_w[...].reshape(-1, half))
         tower_buf[pl.ds(h, n), :, :, 0:half] = out.reshape(n, grid, images, half)
 
-    by_rows(column_step)
+    by_rows(column_step, 8)
 
     group = small
     n_groups = small // group
@@ -631,7 +629,7 @@
             jax.ShapeDtypeStruct((1, width), jnp.float32),
             jax.ShapeDtypeStruct((row_width, col_width), jnp.float32),
         ),
-        in_specs=[pl.BlockSpec(memory_space=pl.ANY)],
+        in_specs=[pl.BlockSpec(memory_space=pltpu.HBM)],
         out_specs=(vmem, vmem),
         scratch_shapes=[
             pltpu.VMEM((images, width), jnp.float32),
@@ -658,7 +656,7 @@
             dma,
         ],
         compiler_params=pltpu.CompilerParams(
-            collective_id=0, has_side_effects=True, vmem_limit_bytes=48 * 1024 * 1024
+            collective_id=0, has_side_effects=True, vmem_limit_bytes=64 * 1024 * 1024 - 64 * 1024
         ),
         name="exchange",
     )(features)

time: 70.2 us -> 71.2 us (1.014)
  local copies, waits for them, and re-layouts: 2.29 us -> 3.16 us
    unnamed x4 -> x2, local copies, waits for them, and re-layouts: 2.29 us -> 3.16 us
where the time goes in v5:
time: 71.2 us; the launch traced here: 71 us
  Pallas kernels  67.1 us (94%)
  local copies, waits for them, and re-layouts  3.16 us (4%)
    pallas_call x1, Pallas kernels, network(): pl.pallas_call(network_kernel, out_shape=jax.ShapeDtypeStruct((images, wi...  41 us
    pallas_call x1, Pallas kernels, exchange(): pl.pallas_call(functools.partial(exchange_kernel, n_sample, n_col), out_s...  26.2 us
    unnamed x2, local copies, waits for them, and re-layouts  3.16 us

profile of v5, /device:TPU:0, one launch (start us, length us, event | category | flops | bytes accessed | tf_op | source)
XLA Modules:
  0.0 71.0 jit_solution(16143429900011511140)
XLA Ops:
  0.6 41.0 %network.1.feats_hbm = f32[16,2048]{1,0:T(8,128)} custom-call(bf16[17,17,16,768]{3,2,1,0:T(8,128)(2,1)} %bitcast.16, bf16[768,384]{1,0:T(8,128)(2,1)} %bitcast.27, bf16[9,192,320]{2,1,0:T(8,128)(2,1)} %bitcast.19, bf16[7,192,192]{2,1,0:T(8,128)(2,1)} %bitcast.25, bf16[7,192,192]{2,1,0:T(8,128)(2,1)} %bitcast.26, bf16[9,192,192]{2,1,0:T(8,128)(2,1)} %bitcast.20, ...), custom_call_target="tpu_custom_call" | custom-call | tf_op jit(solution)/shard_map/network/pallas_call | solution.py:376
  41.6 26.2 %exchange.1 = (f32[1,2048]{1,0:T(1,128)}, f32[256,512]{1,0:T(8,128)}) custom-call(f32[16,2048]{1,0:T(8,128)} %network.1.feats_hbm), custom_call_target="tpu_custom_call" | custom-call | tf_op jit(solution)/shard_map/exchange/pallas_call | solution.py:626
  67.8 1.3 %copy.17 = f32[2048]{0:T(1024)} copy(f32[2048]{0:T(1024)} %bitcast.29) | data formatting | bytes 16384
  69.1 1.9 %copy.18 = f32[256,512]{1,0:T(8,128)} copy(f32[256,512]{1,0:T(8,128)} %get-tuple-element.9) | data formatting | bytes 1048576
